TPU v7x, 32 devices: a whole 2x2x4 slice. The times are simulated.
32 devices in a mesh: table: 16 (over z, y, x), segment: 2 (over core).
Axes of the slice: x: 2, y: 2, z: 4, core: 2. Of those that a mesh axis runs over, the one named last changes fastest.
Arguments:
- hidden: bfloat16 [2, 4096, 1280], P('segment', 'table'), may hold values from -6 to 6
- owner: int32 [2, 4096, 8], P('segment', 'table'), may hold values from 0 to 15, all different within a row; in each aligned block of 256 rows (0 to 255, 256 to 511, ..., all dimensions but the last counted through in order) at most 256 rows name the same one
- slot: int32 [2, 4096, 8], P('segment', 'table'), may hold values from 0 to 511
- memory_table: bfloat16 [2, 8192, 640], P('segment', 'table'), may hold values from -6 to 6
- key_weight: bfloat16 [2, 640, 1280], P('segment'), may hold values from -0.25 to 0.25
- value_weight: bfloat16 [2, 640, 1280], P('segment'), may hold values from -0.25 to 0.25
- conv_weight: float32 [2, 4, 1280], P('segment'), may hold values from -3 to 3
Outputs:
- passed: bfloat16 [2, 4096, 1280], P('segment', 'table')
Inputs may be any that keep to these rules, and one draw needn't show every extreme that they name: `owner`: A token's 8 heads name different shards; among the tokens of one device no shard is named by more than 256 lookups, a bound that some block reaches.
All inputs are finite; a program needn't handle non-finite values.
Results may differ from a plain program's by a relative error of at most 0.0047.
Values may be sent and summed in bfloat16 or wider, within the bound.
A program may use at most 64 MiB of HBM per device.

v0:
```python
import math

import jax
import jax.numpy as jnp
from jax import lax
from jax.sharding import PartitionSpec as P

CONV_DILATION = 3


def shifted(value, axis, by):
    length = lax.axis_size(axis)
    pairs = [(i, i + by) for i in range(length) if 0 <= i + by < length]
    return lax.ppermute(value, axis, pairs)


def passed_along(value, axis, steps):
    count = lax.axis_size(axis)
    pairs = [(source, (source + steps) % count) for source in range(count)]
    return lax.ppermute(value, axis, pairs)


def rms_scale(values):
    return values * lax.rsqrt(jnp.mean(values * values, axis=-1, keepdims=True) + 1e-06)


def local(hidden, owner, slot, memory_table, key_weight, value_weight, conv_weight):
    states = hidden[0]
    owners = owner[0]
    slot_rows = slot[0]
    table_local = memory_table[0]
    tok_rows, head_count = owners.shape
    features = states.shape[1]
    row_count = table_local.shape[0]
    global_ids = owners * row_count + slot_rows
    whole_table = lax.all_gather(table_local, "table", axis=0, tiled=True)
    fetched = whole_table[global_ids]
    memory = jnp.zeros((tok_rows, table_local.shape[1]), jnp.float32)
    for head_index in range(head_count):
        memory = memory + fetched[:, head_index].astype(jnp.float32)
    packed = memory.astype(jnp.bfloat16)
    keys_out = jnp.dot(packed, key_weight[0], preferred_element_type=jnp.float32)
    values_out = jnp.dot(packed, value_weight[0], preferred_element_type=jnp.float32)
    states_float = states.astype(jnp.float32)
    affinity = jnp.sum(
        rms_scale(states_float) * rms_scale(keys_out), axis=-1, keepdims=True
    ) / math.sqrt(features)
    gated_value = jax.nn.sigmoid(affinity) * values_out
    scaled_states = rms_scale(gated_value)
    kernel_taps_count = conv_weight.shape[1]
    receptive_rows = (kernel_taps_count - 1) * CONV_DILATION
    earlier = shifted(
        scaled_states[tok_rows - receptive_rows :].astype(jnp.bfloat16), "table", 1
    ).astype(jnp.float32)
    extended = jnp.concatenate([earlier, scaled_states], axis=0)
    convolved = jnp.zeros((tok_rows, features), jnp.float32)
    for kernel_tap_index in range(kernel_taps_count):
        shifted_rows = receptive_rows - kernel_tap_index * CONV_DILATION
        convolved = (
            convolved
            + conv_weight[0, kernel_tap_index] * extended[shifted_rows : shifted_rows + tok_rows]
        )
    branch_out = jax.nn.silu(convolved) + gated_value
    result = (states_float + branch_out).astype(jnp.bfloat16)
    return passed_along(result, "segment", 1)[None]


def solution(mesh):
    in_specs = (
        P("segment", "table", None),
        P("segment", "table", None),
        P("segment", "table", None),
        P("segment", "table", None),
        P("segment", None, None),
        P("segment", None, None),
        P("segment", None, None),
    )
    out_specs = P("segment", "table", None)
    return jax.shard_map(local, mesh=mesh, in_specs=in_specs, out_specs=out_specs, check_vma=False)
```

profile of v0, /device:TPU:0, one launch (start us, length us, event | category | flops | bytes accessed | tf_op | source)
XLA Modules:
  0.0 192.9 jit_solution(1038833653763821469)
XLA Ops:
  6.5 0.0 copy-start
  6.5 0.0 copy-start.1
  6.5 0.0 all-gather.3.cloned.1.call-start
  6.5 0.7 all-gather.3.cloned.1.call-update
  7.3 0.7 compare_select_fusion
  8.0 0.1 copy.8
  8.1 0.1 reshape.79
  8.2 0.0 copy-done.1
  8.2 0.2 fusion.10
  8.5 136.5 %all-gather.3.cloned.1.call-done = bf16[1,8192,640]{2,1,0:T(8,128)(2,1)} async-done(((bf16[1,512,640]{2,1,0:T(8,128)(2,1)}), bf16[1,8192,640]{2,1,0:T(8,128)(2,1)}) %all-gather.3.cloned.1.call-update) | async-done | bytes 10485776 | tf_op jit(solution)/shard_map/all_gather | solution.py:36
  145.0 14.8 %gather_fusion = bf16[2048,640]{1,0:T(8,128)(2,1)} fusion(bf16[8192,640]{1,0:T(8,128)(2,1)} %bitcast.26, s32[2048]{0:T(1024)S(1)} %broadcast_clamp_fusion), kind=kCustom, calls=%fused_computation | custom fusion | bytes 5251072 | tf_op jit(solution)/shard_map/gather | solution.py:37
  159.8 13.8 %fusion.16 = (bf16[256,1,640]{2,1,0:T(2,128)(2,1)S(1)}, bf16[256,1,640]{2,1,0:T(2,128)(2,1)S(1)}, bf16[256,1,640]{2,1,0:T(2,128)(2,1)S(1)}, bf16[256,1,640]{2,1,...) fusion(bf16[256,8,640]{2,1,0:T(8,128)(2,1)} %bitcast.27), kind=kLoop, calls=%fused_computation.41 | loop fusion | bytes 5242880 | tf_op jit(solution)/shard_map/slice | solution.py:40
  173.6 0.3 fusion.15
  173.9 0.0 copy-done
  173.9 0.8 multiply_reduce_fusion.1
  174.7 0.0 copy-start.2
  174.7 0.4 fusion.12
  175.1 1.0 copy-done.2
  176.1 0.8 multiply_reduce_fusion
  176.9 0.0 copy-start.3
  176.9 0.2 broadcast_multiply_fusion
  177.1 3.4 %collective-permute-start = (bf16[9,1280]{1,0:T(8,128)(2,1)S(1)}, bf16[9,1280]{1,0:T(8,128)(2,1)S(1)}, u32[]{:S(2)}, u32[]{:S(2)}) collective-permute-start(bf16[9,1280]{1,0:T(8,128)(2,1)S(1)} %slice.117), channel_id=1, source_target_pairs={{0,2},{2,4},{4,6},{6,8},{8,10},{10,12},{12,14},{14,16},{16,18},{18... | collective-permute-start | bytes 69128 | tf_op jit(solution)/shard_map/ppermute | solution.py:14
  180.5 0.0 copy-done.3
  180.5 0.1 slice_reduce_fusion.3
  180.5 1.6 collective-permute-done
  182.1 0.9 fusion.13
  183.1 0.1 collective-permute-start.1
  183.1 2.1 %collective-permute-done.1 = bf16[256,1280]{1,0:T(8,128)(2,1)S(1)} collective-permute-done((bf16[256,1280]{1,0:T(8,128)(2,1)S(1)}, bf16[256,1280]{1,0:T(8,128)(2,1)S(1)}, u32[]{:S(2)}, u32[]{:S(2)}) %collective-permute-start.1) | collective-permute-done | bytes 655392 | tf_op jit(solution)/shard_map/ppermute | solution.py:20
  185.2 0.8 copy.34
  (6 shorter events, 0.0 us)
Async XLA Ops:
  6.5 167.4 %copy-start = (bf16[1,640,1280]{2,1,0:T(8,128)(2,1)S(1)}, bf16[1,640,1280]{2,1,0:T(8,128)(2,1)}, u32[]{:S(2)}) copy-start(bf16[1,640,1280]{2,1,0:T(8,128)(2,1)} %param.11) | copy-start | bytes 4915204
  6.5 1.7 copy-start.1
  6.5 138.5 %all-gather.3.cloned.1.call-start = ((), (), s32[]{:S(2)}) async-start(), calls=%async_computation | async-start | bytes 11141120 | tf_op jit(solution)/shard_map/all_gather | solution.py:36
  174.7 1.4 copy-start.2
  176.9 3.6 %copy-start.3 = (f32[1,4,1280]{2,1,0:T(4,128)S(1)}, f32[1,4,1280]{2,1,0:T(4,128)}, u32[]{:S(2)}) copy-start(f32[1,4,1280]{2,1,0:T(4,128)} %param.13) | copy-start | bytes 61444
  177.1 5.0 %collective-permute-start = (bf16[9,1280]{1,0:T(8,128)(2,1)S(1)}, bf16[9,1280]{1,0:T(8,128)(2,1)S(1)}, u32[]{:S(2)}, u32[]{:S(2)}) collective-permute-start(bf16[9,1280]{1,0:T(8,128)(2,1)S(1)} %slice.117), channel_id=1, source_target_pairs={{0,2},{2,4},{4,6},{6,8},{8,10},{10,12},{12,14},{14,16},{16,18},{18... | collective-permute-start | bytes 69128 | tf_op jit(solution)/shard_map/ppermute | solution.py:14
  183.1 2.2 %collective-permute-start.1 = (bf16[256,1280]{1,0:T(8,128)(2,1)S(1)}, bf16[256,1280]{1,0:T(8,128)(2,1)S(1)}, u32[]{:S(2)}, u32[]{:S(2)}) collective-permute-start(bf16[256,1280]{1,0:T(8,128)(2,1)S(1)} %fusion.13), channel_id=1, source_target_pairs={{0,1},{1,0},{2,3},{3,2},{4,5},{5,4},{6,7},{7,6},{8,9},{9,8},{10,11... | collective-permute-start | bytes 1966088 | tf_op jit(solution)/shard_map/ppermute | solution.py:20
Sparse Core Ops, SparseCore 0:
  10.0 134.8 all-gather.2
where the time goes:
time: 194 us; the launch traced here: 193 us
  waiting for transfers between devices  141 us (73%)
  local copies, waits for them, and re-layouts  30.8 us (16%)
  between operations  13.5 us (7%)
  starting transfers between devices  3.43 us (2%)
  other arithmetic  2.67 us (1%)
    all_gather x1, waiting for transfers between devices, local(): whole_table = lax.all_gather(table_local, 'table', axis=0, tiled=True)  137 us
    gather x1, local copies, waits for them, and re-layouts, local(): fetched = whole_table[global_ids]  14.8 us
    slice x1, local copies, waits for them, and re-layouts, local(): memory = memory + fetched[:, head_index].astype(jnp.float32)  13.8 us
  transfers between devices with their start and end apart: 3, of which 3 were waited for; matrix products, arithmetic and copies ran while one was open for 1% of the time, Pallas kernels for 0%

commit v1 on v0

v1 whole, which is shorter than its diff:
```python
import functools
import math

import jax
import jax.numpy as jnp
from jax import lax
from jax.experimental import pallas as pl
from jax.experimental.pallas import tpu as pltpu
from jax.sharding import PartitionSpec as P

CONV_DILATION = 3
PLANE = 4
LANES = 128
HALO = 16
EPS = 1e-06


def kernel(n, n_segment, hidden, owner, slot, table, key_weight, value_weight, taps, out,
           tab, hot, codes, stage, landed, own, packed, hid, kw, vw, tp, keys, values, normed, edge_out, edge_in, res,
           code_s, code_r, own_s, own_r, fwd_s, fwd_r, z_s, z_r, halo_s, halo_r, out_s, out_r, tab_l, in_l):
    me = lax.axis_index("table")
    seg = lax.axis_index("segment")
    groups = n // PLANE
    rows = table.shape[0]
    chunks = table.shape[1] // LANES
    tokens, features = hid.shape
    blocks = out_s.shape[0]
    block = tokens // blocks
    kernel_taps = taps.shape[0]

    near = me + 1 - 2 * (me % 2)
    side = me + 2 - 4 * ((me // 2) % 2)
    diag = side + 1 - 2 * (side % 2)
    after, before = (me + 1) % n, (me + n - 1) % n
    seg_after, seg_before = (seg + 1) % n_segment, (seg + n_segment - 1) % n_segment

    def peer(k):
        return (me + PLANE * k) % n

    def remote(src, dst, send, recv, **where):
        return pltpu.make_async_remote_copy(src_ref=src, dst_ref=dst, send_sem=send, recv_sem=recv,
                                            device_id=where, device_id_type=pl.DeviceIdType.MESH)

    barrier = pltpu.get_barrier_semaphore()
    for other in [near, side, after, before] + [peer(k) for k in range(1, groups)]:
        pl.semaphore_signal(barrier, inc=1, device_id={"table": other}, device_id_type=pl.DeviceIdType.MESH)
    for other in (seg_after, seg_before):
        pl.semaphore_signal(barrier, inc=1, device_id={"segment": other}, device_id_type=pl.DeviceIdType.MESH)

    def fetch(c):
        return pltpu.make_async_copy(table.at[:, pl.ds(c * LANES, LANES)], tab.at[c, pl.ds(0, rows)], tab_l.at[c])

    for c in range(chunks):
        fetch(c).start()
    inputs = [pltpu.make_async_copy(src, dst, in_l.at[i]) for i, (src, dst) in enumerate(
        [(hidden, hid), (key_weight, kw), (value_weight, vw), (taps, tp)])]
    for copy in inputs:
        copy.start()
    codes[0] = owner[...] * rows + slot[...]

    pl.semaphore_wait(barrier, 4 + groups - 1 + 2)

    def code_copy(k):
        return remote(codes.at[0], codes.at[groups - k], code_s.at[k], code_r.at[groups - k], table=peer(k))

    def own_copy(c, q):
        return remote(tab.at[c, pl.ds(0, rows)], tab.at[c, pl.ds(q * rows, rows)],
                      own_s.at[c, q], own_r.at[c, q], table=near if q == 1 else side)

    half = rows // 2

    def fwd_copy(c, q):
        at = 0 if q == 1 else half
        return remote(tab.at[c, pl.ds(q * rows + at, half)], tab.at[c, pl.ds(3 * rows + at, half)],
                      fwd_s.at[c, q], fwd_r.at[c, q], table=side if q == 1 else near)

    def z_copy(c, k):
        return remote(stage.at[c, k], landed.at[c, k], z_s.at[c, k], z_r.at[c, k], table=peer(k))

    def send_own(c):
        if c < chunks:
            fetch(c).wait()
            for q in (1, 2):
                own_copy(c, q).start()

    def forward(c):
        if c < chunks:
            for q in (1, 2):
                own_copy(c, q).wait_recv()
                fwd_copy(c, q).start()

    for k in range(1, groups):
        code_copy(k).start()
    send_own(0)
    send_own(1)

    lane = lax.broadcasted_iota(jnp.int32, (tokens, rows), 1)

    def mark(k):
        found = []
        for shard in (me, near, side, diag):
            offset = codes[k] - shard * rows
            inside = (offset >= 0) & (offset < rows)
            found.append(jnp.sum(jnp.where(inside, offset + 1, 0), axis=0, keepdims=True) - 1)
        column = jnp.concatenate(found + found, axis=0).astype(jnp.float32).T.astype(jnp.int32)
        for q in range(PLANE):
            hot[k, :, q * rows:(q + 1) * rows] = jnp.where(lane == column[:, q:q + 1], 1.0, 0.0).astype(jnp.bfloat16)

    mark(0)
    for k in range(1, groups):
        code_copy(k).wait_recv()

    @pl.loop(1, groups)
    def _(k):
        mark(k)

    forward(0)
    send_own(2)
    for c in range(chunks):
        forward(c + 1)
        send_own(c + 3)
        for q in (1, 2):
            fwd_copy(c, q).wait_recv()

        @pl.loop(1, groups)
        def _(k):
            stage[c, k] = jnp.dot(hot[k], tab[c], preferred_element_type=jnp.float32).astype(jnp.bfloat16)
            z_copy(c, k).start()

        own[c] = jnp.dot(hot[0], tab[c], preferred_element_type=jnp.float32)

    for copy in inputs:
        copy.wait()
    for c in range(chunks):
        for k in range(1, groups):
            z_copy(c, k).wait_recv()
        total = own[c]
        for k in range(1, groups):
            total = total + landed[c, k].astype(jnp.float32)
        packed[:, c * LANES:(c + 1) * LANES] = total.astype(jnp.bfloat16)

    keys[...] = jnp.dot(packed[...], kw[...], preferred_element_type=jnp.float32)
    values[...] = jnp.dot(packed[...], vw[...], preferred_element_type=jnp.float32)

    halo = remote(edge_out, edge_in, halo_s, halo_r, table=after)

    def gates(b):
        here = pl.ds(b * block, block)
        states = hid[here, :].astype(jnp.float32)
        key = keys[here, :]
        value = values[here, :]

        def mean(x):
            return jnp.sum(x, axis=-1, keepdims=True) / features

        affinity = (jnp.sum(states * key, axis=-1, keepdims=True)
                    * lax.rsqrt(mean(states * states) + EPS) * lax.rsqrt(mean(key * key) + EPS)) / math.sqrt(features)
        gated = value * jax.nn.sigmoid(affinity)
        scaled = gated * lax.rsqrt(mean(gated * gated) + EPS)
        normed[pl.ds(HALO + b * block, block), :] = scaled
        values[here, :] = gated
        if b == blocks - 1:
            edge_out[...] = scaled[block - HALO:].astype(jnp.bfloat16)
            halo.start()

    def out_copy(b):
        here = pl.ds(b * block, block)
        return remote(res.at[here, :], out.at[here, :], out_s.at[b], out_r.at[b], segment=seg_after)

    def finish(b):
        here = pl.ds(b * block, block)
        mixed = tp[0:1, :] * normed[pl.ds(HALO + b * block, block), :]
        for tap in range(1, kernel_taps):
            mixed = mixed + tp[tap:tap + 1, :] * normed[pl.ds(HALO + b * block - tap * CONV_DILATION, block), :]
        total = hid[here, :].astype(jnp.float32) + (mixed * jax.nn.sigmoid(mixed) + values[here, :])
        res[here, :] = total.astype(jnp.bfloat16)
        out_copy(b).start()

    gates(blocks - 1)
    for b in range(blocks - 1):
        gates(b)
    for b in range(1, blocks):
        finish(b)
    halo.wait_recv()
    normed[pl.ds(0, HALO), :] = jnp.where(me > 0, edge_in[...].astype(jnp.float32), 0.0)
    finish(0)

    for k in range(1, groups):
        code_copy(k).wait_send()
    for c in range(chunks):
        for q in (1, 2):
            own_copy(c, q).wait_send()
            fwd_copy(c, q).wait_send()
        for k in range(1, groups):
            z_copy(c, k).wait_send()
    halo.wait_send()
    for b in range(blocks):
        out_copy(b).wait()


def local(n, n_segment, hidden, owner, slot, memory_table, key_weight, value_weight, conv_weight):
    tokens, features = hidden.shape[1:]
    heads = owner.shape[2]
    rows, width = memory_table.shape[1:]
    kernel_taps = conv_weight.shape[1]
    groups, chunks, blocks = n // PLANE, width // LANES, 8
    bf, f32 = jnp.bfloat16, jnp.float32
    dma = pltpu.SemaphoreType.DMA
    anywhere, vmem = pl.BlockSpec(memory_space=pl.ANY), pl.BlockSpec(memory_space=pltpu.VMEM)
    result = pl.pallas_call(
        functools.partial(kernel, n, n_segment),
        out_shape=jax.ShapeDtypeStruct((tokens, features), bf),
        in_specs=[anywhere, vmem, vmem, anywhere, anywhere, anywhere, anywhere],
        out_specs=anywhere,
        scratch_shapes=[
            pltpu.VMEM((chunks, PLANE * rows, LANES), bf),
            pltpu.VMEM((groups, tokens, PLANE * rows), bf),
            pltpu.VMEM((groups, heads, tokens), jnp.int32),
            pltpu.VMEM((chunks, groups, tokens, LANES), bf),
            pltpu.VMEM((chunks, groups, tokens, LANES), bf),
            pltpu.VMEM((chunks, tokens, LANES), f32),
            pltpu.VMEM((tokens, width), bf),
            pltpu.VMEM((tokens, features), bf),
            pltpu.VMEM((width, features), bf),
            pltpu.VMEM((width, features), bf),
            pltpu.VMEM((kernel_taps, features), f32),
            pltpu.VMEM((tokens, features), f32),
            pltpu.VMEM((tokens, features), f32),
            pltpu.VMEM((HALO + tokens, features), f32),
            pltpu.VMEM((HALO, features), bf),
            pltpu.VMEM((HALO, features), bf),
            pltpu.VMEM((tokens, features), bf),
            dma((groups,)), dma((groups,)),
            dma((chunks, 3)), dma((chunks, 3)),
            dma((chunks, 3)), dma((chunks, 3)),
            dma((chunks, groups)), dma((chunks, groups)),
            dma, dma,
            dma((blocks,)), dma((blocks,)),
            dma((chunks,)), dma((4,)),
        ],
        compiler_params=pltpu.CompilerParams(collective_id=0, has_side_effects=True, vmem_limit_bytes=48 << 20),
    )(hidden[0], owner[0].T, slot[0].T, memory_table[0], key_weight[0], value_weight[0], conv_weight[0])
    return result[None]


def solution(mesh):
    in_specs = (
        P("segment", "table", None),
        P("segment", "table", None),
        P("segment", "table", None),
        P("segment", "table", None),
        P("segment", None, None),
        P("segment", None, None),
        P("segment", None, None),
    )
    out_specs = P("segment", "table", None)
    step = functools.partial(local, mesh.shape["table"], mesh.shape["segment"])
    return jax.shard_map(step, mesh=mesh, in_specs=in_specs, out_specs=out_specs, check_vma=False)
```

time: 194 us -> 60.7 us (0.31)
  waiting for transfers between devices: 141 us -> 0 us
  Pallas kernels: 0 us -> 52.3 us
  local copies, waits for them, and re-layouts: 30.8 us -> 7.99 us
  between operations: 13.5 us -> 0.02 us
  starting transfers between devices: 3.43 us -> 0 us
  other arithmetic: 2.67 us -> 0 us
    all_gather x1 -> x0, waiting for transfers between devices: 137 us -> none  [local(): whole_table = lax.all_gather(table_local, 'table', axis=0, tiled=True)]
    pallas_call x0 -> x1, Pallas kernels: none -> 52.3 us  [local(): pl.pallas_call(functools.partial(kernel, n, n_segment), out_shape=jax.Sha...]
    gather x1 -> x0, local copies, waits for them, and re-layouts: 14.8 us -> none  [local(): fetched = whole_table[global_ids]]
    slice x3 -> x0, local copies, waits for them, and re-layouts: 13.9 us -> none  [the longest x1 13.8 us: local(): memory = memory + fetched[:, head_index].astype(jnp.float32)]
    unnamed x9 -> x15, local copies, waits for them, and re-layouts: 1.9 us -> 7.99 us
    ppermute x2 -> x0, waiting for transfers between devices: 3.67 us -> none  [the longest x1 2.08 us: passed_along(): return lax.ppermute(value, axis, pairs)]
    ppermute x2 -> x0, starting transfers between devices: 3.42 us -> none  [the longest x1 3.35 us: shifted(): return lax.ppermute(value, axis, pairs)]
  transfers between devices with their start and end apart: 3 -> 0, of which waited for: 3 -> 0; matrix products, arithmetic and copies ran while one was open for 1% -> 0% of each run, Pallas kernels for 0% -> 0%
where the time goes in v1:
time: 60.7 us; the launch traced here: 60.3 us
  Pallas kernels  52.3 us (86%)
  local copies, waits for them, and re-layouts  7.99 us (13%)
    pallas_call x1, Pallas kernels, local(): pl.pallas_call(functools.partial(kernel, n, n_segment), out_shape=jax.Sha...  52.3 us
    unnamed x15, local copies, waits for them, and re-layouts  7.99 us

profile of v1, /device:TPU:0, one launch (start us, length us, event | category | flops | bytes accessed | tf_op | source)
XLA Modules:
  0.0 60.3 jit_solution(270644545924032844)
XLA Ops:
  0.0 0.0 copy-start
  0.0 1.4 %copy-done = bf16[1,640,1280]{2,1,0:T(8,128)(2,1)S(1)} copy-done((bf16[1,640,1280]{2,1,0:T(8,128)(2,1)S(1)}, bf16[1,640,1280]{2,1,0:T(8,128)(2,1)}, u32[]{:S(2)}) %copy-start) | copy-done | bytes 1638424
  1.4 0.0 copy-start.1
  1.4 1.4 %copy-done.1 = bf16[1,640,1280]{2,1,0:T(8,128)(2,1)S(1)} copy-done((bf16[1,640,1280]{2,1,0:T(8,128)(2,1)S(1)}, bf16[1,640,1280]{2,1,0:T(8,128)(2,1)}, u32[]{:S(2)}) %copy-start.1) | copy-done | bytes 1638424
  2.9 0.0 copy-start.2
  2.9 1.1 %copy-done.2 = bf16[1,256,1280]{2,1,0:T(8,128)(2,1)S(1)} copy-done((bf16[1,256,1280]{2,1,0:T(8,128)(2,1)S(1)}, bf16[1,256,1280]{2,1,0:T(8,128)(2,1)}, u32[]{:S(2)}) %copy-start.2) | copy-done | bytes 655384
  4.0 0.0 copy-start.3
  4.0 1.1 %copy-done.3 = bf16[1,512,640]{2,1,0:T(8,128)(2,1)S(1)} copy-done((bf16[1,512,640]{2,1,0:T(8,128)(2,1)S(1)}, bf16[1,512,640]{2,1,0:T(8,128)(2,1)}, u32[]{:S(2)}) %copy-start.3) | copy-done | bytes 655384
  5.0 0.0 copy-start.4
  5.0 0.7 %copy-done.4 = f32[1,4,1280]{2,1,0:T(4,128)S(1)} copy-done((f32[1,4,1280]{2,1,0:T(4,128)S(1)}, f32[1,4,1280]{2,1,0:T(4,128)}, u32[]{:S(2)}) %copy-start.4) | copy-done | bytes 20504
  5.8 0.0 copy-start.5
  5.8 0.7 %copy-done.5 = s32[1,256,8]{1,2,0:T(8,128)S(1)} copy-done((s32[1,256,8]{1,2,0:T(8,128)S(1)}, s32[1,256,8]{1,2,0:T(8,128)}, u32[]{:S(2)}) %copy-start.5) | copy-done | bytes 8216
  6.5 0.0 copy-start.6
  6.5 0.7 %copy-done.6 = s32[1,256,8]{1,2,0:T(8,128)S(1)} copy-done((s32[1,256,8]{1,2,0:T(8,128)S(1)}, s32[1,256,8]{1,2,0:T(8,128)}, u32[]{:S(2)}) %copy-start.6) | copy-done | bytes 8216
  7.2 52.3 %shard_map.73 = bf16[256,1280]{1,0:T(8,128)(2,1)S(1)} custom-call(bf16[256,1280]{1,0:T(8,128)(2,1)S(1)} %bitcast.15, s32[8,256]{1,0:T(8,128)S(1)} %bitcast.18, s32[8,256]{1,0:T(8,128)S(1)} %bitcast.19, bf16[512,640]{1,0:T(8,128)(2,1)S(1)} %bitcast.16, bf16[640,1280]{1,0:T(8,128)(2,1)S(1)} %bitcast.13, bf16[640,1280]{1,0:T(8,128)(2,1)S(1)} %bitcast.14, ...), custom_call_target="tpu_custom_call" | custom-call | tf_op jit(solution)/shard_map/pallas_call | solution.py:210
  59.4 0.8 %copy.9 = bf16[1,256,1280]{2,1,0:T(8,128)(2,1)} copy(bf16[1,256,1280]{2,1,0:T(8,128)(2,1)S(1)} %bitcast.12) | data formatting | bytes 1310720
Async XLA Ops:
  0.0 1.4 %copy-start = (bf16[1,640,1280]{2,1,0:T(8,128)(2,1)S(1)}, bf16[1,640,1280]{2,1,0:T(8,128)(2,1)}, u32[]{:S(2)}) copy-start(bf16[1,640,1280]{2,1,0:T(8,128)(2,1)} %param.11) | copy-start | bytes 4915204
  1.4 1.4 %copy-start.1 = (bf16[1,640,1280]{2,1,0:T(8,128)(2,1)S(1)}, bf16[1,640,1280]{2,1,0:T(8,128)(2,1)}, u32[]{:S(2)}) copy-start(bf16[1,640,1280]{2,1,0:T(8,128)(2,1)} %param.12) | copy-start | bytes 4915204
  2.9 1.1 %copy-start.2 = (bf16[1,256,1280]{2,1,0:T(8,128)(2,1)S(1)}, bf16[1,256,1280]{2,1,0:T(8,128)(2,1)}, u32[]{:S(2)}) copy-start(bf16[1,256,1280]{2,1,0:T(8,128)(2,1)} %param.7) | copy-start | bytes 1966084
  4.0 1.1 %copy-start.3 = (bf16[1,512,640]{2,1,0:T(8,128)(2,1)S(1)}, bf16[1,512,640]{2,1,0:T(8,128)(2,1)}, u32[]{:S(2)}) copy-start(bf16[1,512,640]{2,1,0:T(8,128)(2,1)} %param.10) | copy-start | bytes 1966084
  5.0 0.7 %copy-start.4 = (f32[1,4,1280]{2,1,0:T(4,128)S(1)}, f32[1,4,1280]{2,1,0:T(4,128)}, u32[]{:S(2)}) copy-start(f32[1,4,1280]{2,1,0:T(4,128)} %param.13) | copy-start | bytes 61444
  5.8 0.7 %copy-start.5 = (s32[1,256,8]{1,2,0:T(8,128)S(1)}, s32[1,256,8]{1,2,0:T(8,128)}, u32[]{:S(2)}) copy-start(s32[1,256,8]{1,2,0:T(8,128)} %param.8) | copy-start | bytes 24580
  6.5 0.7 %copy-start.6 = (s32[1,256,8]{1,2,0:T(8,128)S(1)}, s32[1,256,8]{1,2,0:T(8,128)}, u32[]{:S(2)}) copy-start(s32[1,256,8]{1,2,0:T(8,128)} %param.9) | copy-start | bytes 24580

commit v2 on v1

--- a/solution.py
+++ b/solution.py
@@ -16,8 +16,8 @@
 
 
 def kernel(n, n_segment, hidden, owner, slot, table, key_weight, value_weight, taps, out,
-           tab, hot, codes, stage, landed, own, packed, hid, kw, vw, tp, keys, values, normed, edge_out, edge_in, res,
-           code_s, code_r, own_s, own_r, fwd_s, fwd_r, z_s, z_r, halo_s, halo_r, out_s, out_r, tab_l, in_l):
+           tab, hot, codes, stage, landed, own, packed, hid, kw, vw, tp, keys, values, normed, edge_out, edge_in, res, relay, own_code, own_slot,
+           code_s, code_r, own_s, own_r, fwd_s, fwd_r, z_s, z_r, halo_s, halo_r, out_s, out_r, tab_l, in_l, relay_s, relay_r):
     me = lax.axis_index("table")
     seg = lax.axis_index("segment")
     groups = n // PLANE
@@ -34,8 +34,15 @@
     after, before = (me + 1) % n, (me + n - 1) % n
     seg_after, seg_before = (seg + 1) % n_segment, (seg + n_segment - 1) % n_segment
 
+    group = me // PLANE
+    line = groups == 4
+    end = group % 3 == 0
+
     def peer(k):
-        return (me + PLANE * k) % n
+        if not line:
+            return (me + PLANE * k) % n
+        other = {1: group + 1 - 2 * (group % 2), 2: group + 2 - 4 * (group // 2), 3: 3 - group}[k]
+        return other * PLANE + me % PLANE
 
     def remote(src, dst, send, recv, **where):
         return pltpu.make_async_remote_copy(src_ref=src, dst_ref=dst, send_sem=send, recv_sem=recv,
@@ -50,18 +57,23 @@
     def fetch(c):
         return pltpu.make_async_copy(table.at[:, pl.ds(c * LANES, LANES)], tab.at[c, pl.ds(0, rows)], tab_l.at[c])
 
+    inputs = [pltpu.make_async_copy(src, dst, in_l.at[i]) for i, (src, dst) in enumerate(
+        [(owner, own_code), (slot, own_slot), (hidden, hid), (key_weight, kw), (value_weight, vw), (taps, tp)])]
+    for copy in inputs[:2]:
+        copy.start()
     for c in range(chunks):
         fetch(c).start()
-    inputs = [pltpu.make_async_copy(src, dst, in_l.at[i]) for i, (src, dst) in enumerate(
-        [(hidden, hid), (key_weight, kw), (value_weight, vw), (taps, tp)])]
-    for copy in inputs:
+    for copy in inputs[2:]:
         copy.start()
-    codes[0] = owner[...] * rows + slot[...]
+    for copy in inputs[:2]:
+        copy.wait()
+    codes[0] = own_code[...] * rows + own_slot[...]
 
     pl.semaphore_wait(barrier, 4 + groups - 1 + 2)
 
     def code_copy(k):
-        return remote(codes.at[0], codes.at[groups - k], code_s.at[k], code_r.at[groups - k], table=peer(k))
+        there = k if line else groups - k
+        return remote(codes.at[0], codes.at[there], code_s.at[k], code_r.at[there], table=peer(k))
 
     def own_copy(c, q):
         return remote(tab.at[c, pl.ds(0, rows)], tab.at[c, pl.ds(q * rows, rows)],
@@ -76,6 +88,24 @@
 
     def z_copy(c, k):
         return remote(stage.at[c, k], landed.at[c, k], z_s.at[c, k], z_r.at[c, k], table=peer(k))
+
+    def relay_copy(c):
+        return remote(stage.at[c, 3], relay.at[c], relay_s.at[c], relay_r.at[c], table=peer(1))
+
+    def look(c, k):
+        return jnp.dot(hot[k], tab[c], preferred_element_type=jnp.float32)
+
+    def send_sums(c, k):
+        stage[c, k] = look(c, k).astype(jnp.bfloat16)
+        z_copy(c, k).start()
+
+    def send_far(c):
+        if line:
+            @pl.when(jnp.logical_not(end))
+            def _():
+                relay_copy(c).wait_recv()
+                stage[c, 2] = (look(c, 2) + relay[c].astype(jnp.float32)).astype(jnp.bfloat16)
+                z_copy(c, 2).start()
 
     def send_own(c):
         if c < chunks:
@@ -122,25 +152,59 @@
         for q in (1, 2):
             fwd_copy(c, q).wait_recv()
 
-        @pl.loop(1, groups)
-        def _(k):
-            stage[c, k] = jnp.dot(hot[k], tab[c], preferred_element_type=jnp.float32).astype(jnp.bfloat16)
-            z_copy(c, k).start()
-
-        own[c] = jnp.dot(hot[0], tab[c], preferred_element_type=jnp.float32)
-
-    for copy in inputs:
+        if line:
+            @pl.when(end)
+            def _():
+                stage[c, 3] = look(c, 3).astype(jnp.bfloat16)
+                relay_copy(c).start()
+                send_sums(c, 2)
+
+            @pl.when(jnp.logical_not(end))
+            def _():
+                send_sums(c, 3)
+
+            if c > 0:
+                send_far(c - 1)
+            send_sums(c, 1)
+        else:
+            @pl.loop(1, groups)
+            def _(k):
+                send_sums(c, k)
+
+        own[c] = look(c, 0)
+    send_far(chunks - 1)
+
+    for copy in inputs[2:]:
         copy.wait()
-    for c in range(chunks):
-        for k in range(1, groups):
-            z_copy(c, k).wait_recv()
-        total = own[c]
-        for k in range(1, groups):
-            total = total + landed[c, k].astype(jnp.float32)
-        packed[:, c * LANES:(c + 1) * LANES] = total.astype(jnp.bfloat16)
-
-    keys[...] = jnp.dot(packed[...], kw[...], preferred_element_type=jnp.float32)
-    values[...] = jnp.dot(packed[...], vw[...], preferred_element_type=jnp.float32)
+
+    def collect(c):
+        def add(ks):
+            for k in ks:
+                z_copy(c, k).wait_recv()
+            total = own[c]
+            for k in ks:
+                total = total + landed[c, k].astype(jnp.float32)
+            packed[:, c * LANES:(c + 1) * LANES] = total.astype(jnp.bfloat16)
+
+        if line:
+            @pl.when(end)
+            def _():
+                add((1, 2))
+
+            @pl.when(jnp.logical_not(end))
+            def _():
+                add((1, 3, 2))
+        else:
+            add(range(1, groups))
+
+    for c in range(chunks - 1):
+        collect(c)
+    early = (chunks - 1) * LANES
+    for weight, product in ((kw, keys), (vw, values)):
+        product[...] = jnp.dot(packed[:, :early], weight[:early, :], preferred_element_type=jnp.float32)
+    collect(chunks - 1)
+    for weight, product in ((kw, keys), (vw, values)):
+        product[...] += jnp.dot(packed[:, early:], weight[early:, :], preferred_element_type=jnp.float32)
 
     halo = remote(edge_out, edge_in, halo_s, halo_r, table=after)
 
@@ -191,8 +255,16 @@
         for q in (1, 2):
             own_copy(c, q).wait_send()
             fwd_copy(c, q).wait_send()
-        for k in range(1, groups):
+        for k in range(1, 3 if line else groups):
             z_copy(c, k).wait_send()
+        if line:
+            @pl.when(end)
+            def _():
+                relay_copy(c).wait_send()
+
+            @pl.when(jnp.logical_not(end))
+            def _():
+                z_copy(c, 3).wait_send()
     halo.wait_send()
     for b in range(blocks):
         out_copy(b).wait()
@@ -206,11 +278,11 @@
     groups, chunks, blocks = n // PLANE, width // LANES, 8
     bf, f32 = jnp.bfloat16, jnp.float32
     dma = pltpu.SemaphoreType.DMA
-    anywhere, vmem = pl.BlockSpec(memory_space=pl.ANY), pl.BlockSpec(memory_space=pltpu.VMEM)
+    anywhere = pl.BlockSpec(memory_space=pl.ANY)
     result = pl.pallas_call(
         functools.partial(kernel, n, n_segment),
         out_shape=jax.ShapeDtypeStruct((tokens, features), bf),
-        in_specs=[anywhere, vmem, vmem, anywhere, anywhere, anywhere, anywhere],
+        in_specs=[anywhere] * 7,
         out_specs=anywhere,
         scratch_shapes=[
             pltpu.VMEM((chunks, PLANE * rows, LANES), bf),
@@ -230,15 +302,19 @@
             pltpu.VMEM((HALO, features), bf),
             pltpu.VMEM((HALO, features), bf),
             pltpu.VMEM((tokens, features), bf),
+            pltpu.VMEM((chunks, tokens, LANES), bf),
+            pltpu.VMEM((heads, tokens), jnp.int32),
+            pltpu.VMEM((heads, tokens), jnp.int32),
             dma((groups,)), dma((groups,)),
             dma((chunks, 3)), dma((chunks, 3)),
             dma((chunks, 3)), dma((chunks, 3)),
             dma((chunks, groups)), dma((chunks, groups)),
             dma, dma,
             dma((blocks,)), dma((blocks,)),
-            dma((chunks,)), dma((4,)),
+            dma((chunks,)), dma((6,)),
+            dma((chunks,)), dma((chunks,)),
         ],
-        compiler_params=pltpu.CompilerParams(collective_id=0, has_side_effects=True, vmem_limit_bytes=48 << 20),
+        compiler_params=pltpu.CompilerParams(collective_id=0, has_side_effects=True, vmem_limit_bytes=62 << 20),
     )(hidden[0], owner[0].T, slot[0].T, memory_table[0], key_weight[0], value_weight[0], conv_weight[0])
     return result[None]
 

time: 60.7 us -> 50.5 us (0.83)
  local copies, waits for them, and re-layouts: 7.99 us -> 1.97 us
  Pallas kernels: 52.3 us -> 48.3 us
    unnamed x15 -> x1, local copies, waits for them, and re-layouts: 7.99 us -> 1.97 us
    pallas_call x1, Pallas kernels: 52.3 us -> 48.3 us  [local(): pl.pallas_call(functools.partial(kernel, n, n_segment), out_shape=jax.Sha...]
where the time goes in v2:
time: 50.5 us; the launch traced here: 50.3 us
  Pallas kernels  48.3 us (96%)
  local copies, waits for them, and re-layouts  1.97 us (4%)
    pallas_call x1, Pallas kernels, local(): pl.pallas_call(functools.partial(kernel, n, n_segment), out_shape=jax.Sha...  48.3 us
    unnamed x1, local copies, waits for them, and re-layouts  1.97 us

profile of v2, /device:TPU:0, one launch (start us, length us, event | category | flops | bytes accessed | tf_op | source)
XLA Modules:
  0.0 50.3 jit_solution(114626596035184609)
XLA Ops:
  0.0 48.3 %shard_map.73 = bf16[256,1280]{1,0:T(8,128)(2,1)} custom-call(bf16[256,1280]{1,0:T(8,128)(2,1)} %bitcast.15, s32[8,256]{1,0:T(8,128)} %bitcast.18, s32[8,256]{1,0:T(8,128)} %bitcast.19, bf16[512,640]{1,0:T(8,128)(2,1)} %bitcast.16, bf16[640,1280]{1,0:T(8,128)(2,1)} %bitcast.13, bf16[640,1280]{1,0:T(8,128)(2,1)} %bitcast.14, f32[4,1280]{1,0:T(4,128)} %bitcast.17), custom_call_target="tpu_custom_call" | custom-call | tf_op jit(solution)/shard_map/pallas_call | solution.py:282
  48.3 2.0 %copy.9 = bf16[1,256,1280]{2,1,0:T(8,128)(2,1)} copy(bf16[1,256,1280]{2,1,0:T(8,128)(2,1)} %bitcast.12) | data formatting | bytes 1310720

commit v3 on v2

--- a/solution.py
+++ b/solution.py
@@ -137,6 +137,8 @@
             hot[k, :, q * rows:(q + 1) * rows] = jnp.where(lane == column[:, q:q + 1], 1.0, 0.0).astype(jnp.bfloat16)
 
     mark(0)
+    forward(0)
+    send_own(2)
     for k in range(1, groups):
         code_copy(k).wait_recv()
 
@@ -144,8 +146,6 @@
     def _(k):
         mark(k)
 
-    forward(0)
-    send_own(2)
     for c in range(chunks):
         forward(c + 1)
         send_own(c + 3)
@@ -225,7 +225,10 @@
         values[here, :] = gated
         if b == blocks - 1:
             edge_out[...] = scaled[block - HALO:].astype(jnp.bfloat16)
-            halo.start()
+
+            @pl.when(me < n - 1)
+            def _():
+                halo.start()
 
     def out_copy(b):
         here = pl.ds(b * block, block)
@@ -245,8 +248,16 @@
         gates(b)
     for b in range(1, blocks):
         finish(b)
-    halo.wait_recv()
-    normed[pl.ds(0, HALO), :] = jnp.where(me > 0, edge_in[...].astype(jnp.float32), 0.0)
+
+    @pl.when(me > 0)
+    def _():
+        halo.wait_recv()
+        normed[pl.ds(0, HALO), :] = edge_in[...].astype(jnp.float32)
+
+    @pl.when(me == 0)
+    def _():
+        normed[pl.ds(0, HALO), :] = jnp.zeros((HALO, features), jnp.float32)
+
     finish(0)
 
     for k in range(1, groups):
@@ -265,7 +276,11 @@
             @pl.when(jnp.logical_not(end))
             def _():
                 z_copy(c, 3).wait_send()
-    halo.wait_send()
+
+    @pl.when(me < n - 1)
+    def _():
+        halo.wait_send()
+
     for b in range(blocks):
         out_copy(b).wait()
 

time: 50.5 us -> 47 us (0.931)
  the two profiles are of different devices: /device:TPU:0 before, /device:TPU:5 now
where the time goes in v3:
time: 47 us; the launch traced here: 46.8 us
  Pallas kernels  44.9 us (96%)
  local copies, waits for them, and re-layouts  1.97 us (4%)
    pallas_call x1, Pallas kernels, local(): pl.pallas_call(functools.partial(kernel, n, n_segment), out_shape=jax.Sha...  44.9 us
    unnamed x1, local copies, waits for them, and re-layouts  1.97 us

profile of v3, /device:TPU:5, one launch (start us, length us, event | category | flops | bytes accessed | tf_op | source)
XLA Modules:
  0.0 46.8 jit_solution(9367223928431383922)
XLA Ops:
  0.0 44.9 %shard_map.73 = bf16[256,1280]{1,0:T(8,128)(2,1)} custom-call(bf16[256,1280]{1,0:T(8,128)(2,1)} %bitcast.15, s32[8,256]{1,0:T(8,128)} %bitcast.18, s32[8,256]{1,0:T(8,128)} %bitcast.19, bf16[512,640]{1,0:T(8,128)(2,1)} %bitcast.16, bf16[640,1280]{1,0:T(8,128)(2,1)} %bitcast.13, bf16[640,1280]{1,0:T(8,128)(2,1)} %bitcast.14, f32[4,1280]{1,0:T(4,128)} %bitcast.17), custom_call_target="tpu_custom_call" | custom-call | tf_op jit(solution)/shard_map/pallas_call | solution.py:297
  44.9 2.0 %copy.9 = bf16[1,256,1280]{2,1,0:T(8,128)(2,1)} copy(bf16[1,256,1280]{2,1,0:T(8,128)(2,1)} %bitcast.12) | data formatting | bytes 1310720
